TPU v7x, 256 devices: a whole 4x4x8 slice. The times are simulated.
256 devices in a mesh: dp: 16 (over x, y_lo, core), mp: 16 (over y_hi, z).
Axes of the slice: x: 4, y: 4 (y_hi: 2, y_lo: 2; y = y_hi * 2 + y_lo), z: 8, core: 2. Of those that a mesh axis runs over, the one named last changes fastest.
Arguments:
- tokens: bfloat16 [4096, 6144], P('dp', 'mp'), may hold values from -36 to 36
- w_qkv: bfloat16 [6144, 12288], P('dp', 'mp'), may hold values from -0.078125 to 0.078125
- out_grad: bfloat16 [4096, 4096], P('dp', 'mp'), may hold values from -24 to 24
Outputs:
- attended: bfloat16 [4096, 4096], P('dp', 'mp')
- grad_tokens: float32 [4096, 6144], P('dp', 'mp')
- grad_qkv: bfloat16 [6144, 12288], P('dp', 'mp')
All inputs are finite; a program needn't handle non-finite values.
Results may differ from a plain program's by a relative error of at most 0.023.
Values may be sent and summed in bfloat16 or wider, within the bound.
A program may use at most 128 MiB of HBM per device.

v0:
```python
import jax
import jax.numpy as jnp
from jax import lax
from jax.sharding import PartitionSpec as P

HD = 128
SEQ = 256


def normalize_rows(values_in):
    as_float = values_in.astype(jnp.float32)
    centred = as_float - jnp.mean(as_float, axis=-1, keepdims=True)
    inv_scale = lax.rsqrt(jnp.mean(centred * centred, axis=-1, keepdims=True) + 1e-06)
    return (centred * inv_scale, inv_scale)


def attention(packed):
    head_count = packed.shape[1] // (3 * HD)
    shaped = packed.reshape(-1, SEQ, head_count, 3, HD)
    query_unit, _ = normalize_rows(shaped[:, :, :, 0, :])
    key_unit, _ = normalize_rows(shaped[:, :, :, 1, :])
    value_rows = shaped[:, :, :, 2, :]
    scores = jnp.einsum(
        "bqhd,bkhd->bhqk", query_unit, key_unit, precision=lax.Precision.HIGHEST
    ) / jnp.sqrt(jnp.float32(HD))
    weights = jnp.exp(scores)
    probs = weights / jnp.sum(weights, axis=-1, keepdims=True)
    result = jnp.einsum("bhqk,bkhd->bqhd", probs, value_rows, precision=lax.Precision.HIGHEST)
    return result.reshape(packed.shape[0], head_count * HD)


def per_device(tokens, w_qkv, out_grad):
    own_width = tokens.shape[1]
    gathered = lax.all_gather(tokens, "mp", axis=1, tiled=True)
    unit, inv_scale = normalize_rows(gathered)
    normed = unit.astype(jnp.bfloat16)
    weights = lax.all_gather(w_qkv, "dp", axis=0, tiled=True)
    projected = jnp.dot(normed, weights, preferred_element_type=jnp.float32)
    qkv = projected.astype(jnp.bfloat16)
    attended, pullback = jax.vjp(attention, qkv.astype(jnp.float32))
    d_qkv = pullback(out_grad.astype(jnp.float32))[0].astype(jnp.bfloat16)
    grad_local = lax.psum_scatter(
        lax.dot_general(
            normed, d_qkv, (((0,), (0,)), ((), ())), preferred_element_type=jnp.float32
        ).astype(jnp.bfloat16),
        "dp",
        scatter_dimension=0,
        tiled=True,
    )
    back_term = lax.dot_general(
        d_qkv, weights, (((1,), (1,)), ((), ())), preferred_element_type=jnp.float32
    )
    d_normed = lax.psum(back_term.astype(jnp.bfloat16), "mp").astype(jnp.float32)
    grad_full = inv_scale * (
        d_normed
        - jnp.mean(d_normed, axis=-1, keepdims=True)
        - unit * jnp.mean(d_normed * unit, axis=-1, keepdims=True)
    )
    grad_tokens = lax.dynamic_slice_in_dim(
        grad_full, lax.axis_index("mp") * own_width, own_width, 1
    )
    return (attended.astype(jnp.bfloat16), grad_tokens, grad_local)


def solution(mesh):
    placed = (P("dp", "mp"), P("dp", "mp"), P("dp", "mp"))
    return jax.shard_map(
        per_device,
        mesh=mesh,
        in_specs=placed,
        out_specs=(P("dp", "mp"), P("dp", "mp"), P("dp", "mp")),
        check_vma=False,
    )
```

profile of v0, /device:TPU:1, one launch (start us, length us, event | category | flops | bytes accessed | tf_op | source)
XLA Modules:
  0.0 471.0 jit_solution(7634970815034040910)
XLA Ops:
  7.2 0.0 all-gather.3.cloned.1.call-start
  7.2 0.7 all-gather.3.cloned.1.call-update
  7.9 0.0 all-gather.5.cloned.1.call-start
  7.9 0.7 all-gather.5.cloned.1.call-update
  8.6 0.0 all-reduce.5.cloned.1.call-start
  8.7 1.7 copy.37
  10.4 96.0 %all-gather.3.cloned.1.call-done = bf16[256,6144]{1,0:T(8,128)(2,1)} async-done(((bf16[256,384]{1,0:T(8,128)(2,1)}), bf16[256,6144]{1,0:T(8,128)(2,1)}) %all-gather.3.cloned.1.call-update) | async-done | bytes 3145744 | tf_op jit(solution)/shard_map/all_gather | solution.py:34
  106.3 2.5 convert_reduce_fusion
  108.9 2.9 fusion.2
  111.8 56.1 %all-gather.5.cloned.1.call-done = bf16[6144,768]{1,0:T(8,128)(2,1)} async-done(((bf16[384,768]{1,0:T(8,128)(2,1)}), bf16[6144,768]{1,0:T(8,128)(2,1)}) %all-gather.5.cloned.1.call-update) | async-done | bytes 9437200 | tf_op jit(solution)/shard_map/all_gather | solution.py:37
  167.9 7.1 %fusion.6 = bf16[256,768]{1,0:T(8,128)(2,1)} fusion(bf16[6144,768]{1,0:T(8,128)(2,1)} %all-gather.5.cloned.1.call-done, bf16[256,6144]{1,0:T(8,128)(2,1)S(1)} %copy-done, f32[256]{0:T(256)S(1)} %add_rsqrt_fusion, f32[256]{0:T(256)S(1)} %broadcast_multiply_fusion.4), kind=kOutput, calls=%fused_computation.12 | convolution fusion | flops 2422407168 | bytes 12978176 | tf_op jit(solution)/shard_map/dot_general | solution.py:38
  174.9 1.2 copy.17
  176.1 0.1 fusion.41
  176.3 0.1 multiply_reduce_fusion.4
  176.4 0.7 fusion.42
  177.1 1.6 convolution_bitcast_fusion.2
  178.7 1.7 fusion.11
  180.4 0.5 convolution_bitcast_fusion
  181.0 0.8 multiply_reduce_fusion.2
  181.8 0.1 fusion.33
  181.9 0.1 add_bitcast_fusion.1
  182.2 4.1 convolution_convert_fusion.1
  186.3 0.2 reduce-scatter.2.cloned.1.call-start
  186.5 5.4 %convolution_convert_fusion = bf16[6144,768]{1,0:T(8,128)(2,1)} fusion(bf16[256,768]{0,1:T(8,128)(2,1)S(1)} %bitcast.100, bf16[256,6144]{1,0:T(8,128)(2,1)S(1)} %copy-done, f32[256]{0:T(256)S(1)} %add_rsqrt_fusion, f32[256]{0:T(256)S(1)} %broadcast_multiply_fusion.4), kind=kOutput, calls=%fused_computation | convolution fusion | flops 2426929152 | bytes 12978176 | tf_op jit(solution)/shard_map/dot_general | solution.py:43
  192.0 1.5 convolution_convert_fusion.2
  193.4 0.8 copy.29
  194.2 152.0 %all-reduce.5.cloned.1.call-done = bf16[256,6144]{1,0:T(8,128)(2,1)} async-done(((bf16[256,6144]{1,0:T(8,128)(2,1)}), bf16[256,6144]{1,0:T(8,128)(2,1)}) %all-reduce.5.cloned.1.call-update) | async-done | bytes 3145744 | tf_op jit(solution)/shard_map/psum | solution.py:53
  346.2 2.8 convert_element_type.48
  348.9 0.1 copy-done.1
  349.0 2.0 convert_reduce_fusion.1
  351.0 0.9 fusion.13
  352.0 112.5 %reduce-scatter.2.cloned.1.call-done = bf16[384,768]{1,0:T(8,128)(2,1)} async-done(((bf16[6144,768]{1,0:T(8,128)(2,1)}), bf16[384,768]{1,0:T(8,128)(2,1)}) %reduce-scatter.2.cloned.1.call-update) | async-done | bytes 589840 | tf_op jit(solution)/shard_map/reduce_scatter | solution.py:42
  (27 shorter events, 0.3 us)
Async XLA Ops:
  7.2 99.2 %all-gather.3.cloned.1.call-start = ((), (), s32[]{:S(2)}) async-start(), calls=%async_computation.1 | async-start | bytes 3342336 | tf_op jit(solution)/shard_map/all_gather | solution.py:34
  7.9 160.0 %all-gather.5.cloned.1.call-start = ((), (), s32[]{:S(2)}) async-start(), calls=%async_computation.2 | async-start | bytes 10027008 | tf_op jit(solution)/shard_map/all_gather | solution.py:37
  8.6 337.5 %all-reduce.5.cloned.1.call-start = ((), (), s32[]{:S(2)}) async-start(), calls=%async_computation.3 | async-start | bytes 6291456 | tf_op jit(solution)/shard_map/psum | solution.py:53
  106.3 61.5 %copy-start = (bf16[256,6144]{1,0:T(8,128)(2,1)S(1)}, bf16[256,6144]{1,0:T(8,128)(2,1)}, u32[]{:S(2)}) copy-start(bf16[256,6144]{1,0:T(8,128)(2,1)} %all-gather.3.cloned.1.call-done) | copy-start | bytes 9437188
  176.2 4.2 copy-start.3
  177.1 5.1 %copy-start.2 = (f32[2,256,256]{1,2,0:T(8,128)}, f32[2,256,256]{1,2,0:T(8,128)S(1)}, u32[]{:S(2)}) copy-start(f32[2,256,256]{1,2,0:T(8,128)S(1)} %get-tuple-element.25) | copy-start | bytes 1572868
  177.1 5.1 %copy-start.4 = (bf16[6144,768]{1,0:T(8,128)(2,1)S(1)}, bf16[6144,768]{1,0:T(8,128)(2,1)}, u32[]{:S(2)}) copy-start(bf16[6144,768]{1,0:T(8,128)(2,1)} %all-gather.5.cloned.1.call-done) | copy-start | bytes 28311556
  186.3 278.2 %reduce-scatter.2.cloned.1.call-start = ((), (), s32[]{:S(2)}) async-start(), calls=%async_computation.4 | async-start | bytes 10027008 | tf_op jit(solution)/shard_map/reduce_scatter | solution.py:42
  346.2 2.8 copy-start.1
Sparse Core Ops, SparseCore 0:
  10.5 95.8 all-gather.2
  108.2 59.6 all-gather.4
  186.4 159.6 all-reduce.4
  349.2 115.2 reduce-scatter.1
where the time goes:
time: 472 us; the launch traced here: 471 us
  waiting for transfers between devices  418 us (89%)
  matrix products  23.3 us (5%)
  between operations  14 us (3%)
  other arithmetic  11.7 us (2%)
    psum x1, waiting for transfers between devices, per_device(): lax.psum(back_term.astype(jnp.bfloat16), 'mp').astype(jnp.float32)  152 us
    reduce_scatter x1, waiting for transfers between devices, per_device(): lax.psum_scatter(lax.dot_general(normed, d_qkv, (((0,), (0,)), ((), ())),...  112 us
    all_gather x1, waiting for transfers between devices, per_device(): gathered = lax.all_gather(tokens, 'mp', axis=1, tiled=True)  96 us
    all_gather x1, waiting for transfers between devices, per_device(): weights = lax.all_gather(w_qkv, 'dp', axis=0, tiled=True)  56.1 us
  transfers between devices with their start and end apart: 4, of which 4 were waited for; matrix products, arithmetic and copies ran while one was open for 4% of the time, Pallas kernels for 0%

commit v1 on v0

v1 whole, which is shorter than its diff:
```python
import jax
import jax.numpy as jnp
from jax import lax
from jax.experimental import pallas as pl
from jax.experimental.pallas import tpu as pltpu
from jax.sharding import PartitionSpec as P

HD = 128
EPS = 1e-06
F32 = jnp.float32
BF16 = jnp.bfloat16
MESH = pl.DeviceIdType.MESH


def mm(a, b, dims, precision=None):
    return lax.dot_general(
        a, b, (dims, ((), ())), preferred_element_type=F32, precision=precision
    )


def normalize(v):
    centred = v - jnp.mean(v, axis=-1, keepdims=True)
    inv = lax.rsqrt(jnp.mean(centred * centred, axis=-1, keepdims=True) + EPS)
    return centred * inv, inv


def normalize_back(d, unit, inv):
    return inv * (
        d
        - jnp.mean(d, axis=-1, keepdims=True)
        - unit * jnp.mean(d * unit, axis=-1, keepdims=True)
    )


def one_head(q, k, v, og):
    qu, qi = normalize(q.astype(F32))
    ku, ki = normalize(k.astype(F32))
    scale = 1.0 / (HD**0.5)
    scores = mm(qu, ku, ((1,), (1,)), lax.Precision.HIGHEST) * scale
    weights = jnp.exp(scores)
    probs = weights / jnp.sum(weights, axis=-1, keepdims=True)
    probs16 = probs.astype(BF16)
    out = mm(probs16, v, ((1,), (0,)))
    dv = mm(probs16, og, ((0,), (0,)))
    dp = mm(og, v, ((1,), (1,)))
    ds = (probs * (dp - jnp.sum(dp * probs, axis=-1, keepdims=True)) * scale).astype(BF16)
    dq = normalize_back(mm(ds, ku.astype(BF16), ((1,), (0,))), qu, qi)
    dk = normalize_back(mm(ds, qu.astype(BF16), ((0,), (0,))), ku, ki)
    return out, dq, dk, dv


def kernel(
    tok_ref, w_ref, og_ref,
    att_ref, gt_ref, gw_ref,
    wfull, tfull, normed, normt, acc, qkv, dqkv,
    gown, gout, gin, gya, gxq, gxh, gyb,
    bk, bh, bw, by, stat_out, stat_in,
    send_sem, recv_sem, stat_send, stat_recv,
):
    dp, mp = lax.axis_index("dp"), lax.axis_index("mp")
    x, y, c = dp // 4, (dp // 2) % 2, dp % 2
    yh, z = mp // 8, mp % 8
    rows, width = tok_ref.shape
    depth = w_ref.shape[0]
    half, quarter = depth // 2, depth // 4
    hrow = rows // 2

    def ring(v, d, n):
        return lax.rem(v + d + n, n)

    sib = {"dp": dp + 1 - 2 * c}
    ydev = {"dp": x * 4 + (1 - y) * 2 + c}
    xdev = {d: {"dp": ring(x, d, 4) * 4 + y * 2 + c} for d in (1, -1)}
    zdev = {d: {"mp": yh * 8 + ring(z, d, 8)} for d in (1, -1)}
    yhdev = {"mp": (1 - yh) * 8 + z}
    peers = [{"mp": lax.rem(mp + d, 16)} for d in range(1, 16)]

    barrier = pltpu.get_barrier_semaphore()
    everyone = [sib, ydev, xdev[1], xdev[-1]] + peers
    for dev in everyone:
        pl.semaphore_signal(barrier, inc=1, device_id=dev, device_id_type=MESH)
    pl.semaphore_wait(barrier, len(everyone))

    started = []

    def send(src, dst, dev):
        n = len(started)
        cp = pltpu.make_async_remote_copy(
            src_ref=src, dst_ref=dst, send_sem=send_sem.at[n], recv_sem=recv_sem.at[n],
            device_id=dev, device_id_type=MESH,
        )
        cp.start()
        started.append(cp)
        return cp

    def wp(xd, yd, r0, n, core=None):
        core = c if core is None else core
        r = pl.multiple_of(core * depth + r0, 16)
        return wfull.at[ring(x, xd, 4) * 2 + yd, pl.ds(r, n), :]

    def wsend(xd, yd, r0, n, dev):
        return send(wp(xd, yd, r0, n), wp(xd, yd, r0, n), dev)

    def wown(r0, n, dev):
        return send(w_ref.at[pl.ds(r0, n), :], wp(0, y, r0, n), dev)

    def tp(yb, zd, r0=0, n=rows):
        return tfull.at[yb * 8 + ring(z, zd, 8), pl.ds(r0, n), :]

    def tsend(yb, zd, r0, n, dev):
        return send(tp(yb, zd, r0, n), tp(yb, zd, r0, n), dev)

    to_sib = []
    yo = 1 - y
    t_yh = send(tok_ref, tp(yh, 0), yhdev)
    t_own = {d: send(tok_ref, tp(yh, 0), zdev[d]) for d in (1, -1)}
    b_y = wown(half, half, ydev)
    a_x = {d: wown(0, half, xdev[d]) for d in (1, -1)}
    a_y = wown(0, half, ydev)
    b_x = {d: wown(half, half, xdev[d]) for d in (1, -1)}
    to_sib.append(wown(0, depth, sib))

    def column_to_rows(parts):
        lane = lax.broadcasted_iota(jnp.int32, (rows, 128), 1)
        tile = jnp.zeros((rows, 128), F32)
        for i, p in enumerate(parts):
            tile = jnp.where(lane == i, p, tile)
        return jnp.transpose(tile)[:8, :]

    def rows_to_columns(r):
        return jnp.transpose(jnp.concatenate([r, jnp.zeros((120, rows), F32)], axis=0))

    def exchange(which, parts):
        stat_out[which] = column_to_rows(parts)
        stat_in[which, mp] = stat_out[which]
        cps = []
        for d in range(1, 16):
            cp = pltpu.make_async_remote_copy(
                src_ref=stat_out.at[which], dst_ref=stat_in.at[which, mp],
                send_sem=stat_send.at[which, d], recv_sem=stat_recv.at[which, d],
                device_id=peers[d - 1], device_id_type=MESH,
            )
            cp.start()
            cps.append(cp)
        return cps

    own = tok_ref[...].astype(F32)
    local_mean = jnp.mean(own, axis=-1, keepdims=True)
    local_dev = own - local_mean
    stats = exchange(0, (local_mean, jnp.sum(local_dev * local_dev, axis=-1, keepdims=True)))
    tfull[mp] = tok_ref[...]
    wfull[x * 2 + y, pl.ds(pl.multiple_of(c * depth, 16), depth), :] = w_ref[...]

    t_in = {(0, d): t_own[d] for d in (1, -1)}
    t_yh.wait_recv()
    for d in (1, -1):
        t_in[(1, d)] = tsend(1 - yh, 0, 0, rows, zdev[d])

    def t_hop(h, rel):
        yb = yh if rel == 0 else 1 - yh
        for d in (1, -1):
            t_in[(rel, d)].wait_recv()
        for d in (1, -1):
            if h < 3:
                t_in[(rel, d)] = tsend(yb, -d * h, 0, rows, zdev[d])
            elif h == 3:
                t_in[(rel, d)] = tsend(yb, -d * h, 0 if d == 1 else hrow, hrow, zdev[d])

    t_hop(1, 0)
    b_y.wait_recv()
    bo_x = {d: wsend(0, yo, half, half, xdev[d]) for d in (1, -1)}
    to_sib.append(wsend(0, yo, half, half, sib))
    aq_x, ay_x = {}, {}
    for d in (1, -1):
        a_x[d].wait_recv()
        aq_x[d] = wsend(-d, y, 0 if d == 1 else quarter, quarter, xdev[d])
        ay_x[d] = wsend(-d, y, 0, half, ydev)
        to_sib.append(wsend(-d, y, 0, half, sib))
    t_hop(1, 1)
    a_y.wait_recv()
    to_sib.append(wsend(0, yo, 0, half, sib))
    bq_x, boq_x = {}, {}
    for d in (1, -1):
        b_x[d].wait_recv()
        bq_x[d] = wsend(-d, y, half + (0 if d == 1 else quarter), quarter, xdev[d])
        to_sib.append(wsend(-d, y, half, half, sib))
    t_hop(2, 0)
    ayq = {}
    for d in (1, -1):
        aq_x[d].wait_recv()
        r0 = 0 if d == 1 else quarter
        ayq[d] = wsend(-2 * d, y, r0, quarter, ydev)
        to_sib.append(wsend(-2 * d, y, r0, quarter, sib))
    t_hop(2, 1)
    for d in (1, -1):
        bo_x[d].wait_recv()
        boq_x[d] = wsend(-d, yo, half + (0 if d == 1 else quarter), quarter, xdev[d])
        to_sib.append(wsend(-d, yo, half, half, sib))
    t_hop(3, 0)
    for d in (1, -1):
        bq_x[d].wait_recv()
        to_sib.append(wsend(-2 * d, y, half + (0 if d == 1 else quarter), quarter, sib))
    for d in (1, -1):
        ay_x[d].wait_recv()
        to_sib.append(wsend(-d, yo, 0, half, sib))
    t_hop(3, 1)
    for d in (1, -1):
        boq_x[d].wait_recv()
        to_sib.append(wsend(-2 * d, yo, half + (0 if d == 1 else quarter), quarter, sib))
    for d in (1, -1):
        ayq[d].wait_recv()
        to_sib.append(wsend(-2 * d, yo, 0 if d == 1 else quarter, quarter, sib))

    for cp in stats:
        cp.wait_recv()
    means = stat_in[0, :, 0:1, :]
    mean_row = jnp.mean(means, axis=0)
    sq = jnp.sum(stat_in[0, :, 1:2, :], axis=0) + width * jnp.sum(
        (means - mean_row[None]) * (means - mean_row[None]), axis=0
    )
    inv_row = lax.rsqrt(sq / (16.0 * width) + EPS)
    both = rows_to_columns(jnp.concatenate([mean_row, inv_row, jnp.zeros((6, rows), F32)], axis=0))
    mean, inv = both[:, 0:1], both[:, 1:2]

    t_hop(4, 0)
    t_hop(4, 1)
    for cp in to_sib:
        cp.wait_recv()

    acc[...] = jnp.zeros_like(acc)

    @pl.loop(0, 8)
    def _(k):
        for s in range(2):
            unit = ((tfull[2 * k + s].astype(F32) - mean) * inv).astype(BF16)
            normed[k, :, s * width : (s + 1) * width] = unit
            normt[2 * k + s] = jnp.transpose(unit)
        acc[...] += mm(normed[k], wfull[k], ((1,), (0,)))

    qkv[...] = acc[...].astype(BF16)

    for h in range(2):
        base = 3 * h * HD
        parts = [qkv[:, base + i * HD : base + (i + 1) * HD] for i in range(3)]
        out, dq, dk, dv = one_head(*parts, og_ref[:, h * HD : (h + 1) * HD])
        att_ref[:, h * HD : (h + 1) * HD] = out.astype(BF16)
        for i, g in enumerate((dq, dk, dv)):
            dqkv[:, base + i * HD : base + (i + 1) * HD] = g.astype(BF16)

    def back(yb, zd):
        j = yb * 8 + ring(z, zd, 8)
        w = wfull[j // 2, pl.ds(pl.multiple_of((j % 2) * depth, 16), depth), :]
        bk[j] = mm(dqkv[...], w, ((1,), (1,))).astype(BF16)

    def bp(yb, zd, r0=0, n=rows):
        return bk.at[yb * 8 + ring(z, zd, 8), pl.ds(r0, n), :]

    ybs = (1 - yh, yh)
    b_in = {}

    def back_start():
        for r in range(2):
            back(ybs[r], 4)
            for i, d in enumerate((1, -1)):
                b_in[(r, d)] = send(bp(ybs[r], 4, i * hrow, hrow), bh.at[r, i], zdev[d])

    def back_hop(h, r):
        for i, d in enumerate((1, -1)):
            back(ybs[r], d * (4 - h))
        for i, d in enumerate((1, -1)):
            b_in[(r, d)].wait_recv()
            if h == 1:
                dst = bp(ybs[r], d * 3, i * hrow, hrow)
                dst[...] = (dst[...].astype(F32) + bh[r, i].astype(F32)).astype(BF16)
            else:
                dst = bp(ybs[r], d * (4 - h))
                dst[...] = (dst[...].astype(F32) + bw[r, i, h - 2].astype(F32)).astype(BF16)
            b_in[(r, d)] = send(bp(ybs[r], d * (4 - h)), bw.at[r, i, h - 1], zdev[d])

    g_sib = {}

    def chip(xd, yd):
        return ring(x, xd, 4) * 2 + yd

    def grad(xd, yd):
        q = chip(xd, yd)
        gout[q] = mm(normt[2 * q + 1 - c], dqkv[...], ((1,), (0,))).astype(BF16)
        g_sib[(xd, yd is yo)] = send(gout.at[q], gin.at[q], sib)
        gown[q] = mm(normt[2 * q + c], dqkv[...], ((1,), (0,))).astype(BF16)

    def join(xd, yd):
        q = chip(xd, yd)
        g_sib[(xd, yd is yo)].wait_recv()
        gown[q] = (gown[q].astype(F32) + gin[q].astype(F32)).astype(BF16)

    def gp(xd, yd, r0, n):
        return gown.at[chip(xd, yd), pl.ds(r0, n), :]

    def add(dst, src):
        dst[...] = (dst[...].astype(F32) + src[...].astype(F32)).astype(BF16)

    back_start()
    grad(2, yo)
    grad(2, y)
    back_hop(1, 0)
    grad(1, yo)
    grad(-1, yo)
    back_hop(1, 1)
    ga_y, gq, gh = {}, {}, {}
    for i, yd in enumerate((yo, y)):
        join(2, yd)
        if i == 0:
            ga_y[2] = send(gp(2, yo, 0, half), gya.at[0], ydev)
        for s, d in enumerate((1, -1)):
            gq[(i, d)] = send(gp(2, yd, half + s * quarter, quarter), gxq.at[i, s], xdev[d])
    grad(0, yo)
    for s, d in enumerate((1, -1)):
        join(d, yo)
        ga_y[d] = send(gp(d, yo, 0, half), gya.at[1 + s], ydev)
    grad(1, y)
    grad(-1, y)
    join(0, yo)
    ga_y[0] = send(gp(0, yo, 0, half), gya.at[3], ydev)
    back_hop(2, 0)
    for d in (1, -1):
        join(d, y)
    back_hop(2, 1)
    for i, yd in enumerate((yo, y)):
        for s, d in enumerate((1, -1)):
            gq[(i, d)].wait_recv()
            add(gp(d, yd, half + s * quarter, quarter), gxq.at[i, s])
            gh[(i, d)] = send(gp(d, yd, half, half), gxh.at[i, s], xdev[d])
    grad(0, y)
    join(0, y)
    ga_y[2].wait_recv()
    add(gp(2, y, 0, half), gya.at[0])
    for s, d in enumerate((1, -1)):
        gq[(2, d)] = send(gp(2, y, s * quarter, quarter), gxq.at[2, s], xdev[d])
    back_hop(3, 0)
    back_hop(3, 1)
    for s, d in enumerate((1, -1)):
        ga_y[d].wait_recv()
        add(gp(d, y, 0, half), gya.at[1 + s])
        gq[(2, d)].wait_recv()
        add(gp(d, y, s * quarter, quarter), gxq.at[2, s])
        gh[(2, d)] = send(gp(d, y, 0, half), gxh.at[2, s], xdev[d])
    for s, d in enumerate((1, -1)):
        gh[(0, d)].wait_recv()
        add(gp(0, yo, half, half), gxh.at[0, s])
    gb_y = send(gp(0, yo, half, half), gyb, ydev)
    ga_y[0].wait_recv()
    add(gp(0, y, 0, half), gya.at[3])

    back(ybs[0], 0)
    back(ybs[1], 0)
    for i, d in enumerate((1, -1)):
        b_in[(0, d)].wait_recv()
        add(bp(ybs[0], 0), bw.at[0, i, 2])
    b_y2 = send(bp(ybs[0], 0), by, yhdev)
    for i, d in enumerate((1, -1)):
        b_in[(1, d)].wait_recv()
    d_normed = (
        bk[mp].astype(F32) + bw[1, 0, 2].astype(F32) + bw[1, 1, 2].astype(F32)
    )
    b_y2.wait_recv()
    d_normed = d_normed + by[...].astype(F32)
    unit = (tok_ref[...].astype(F32) - mean) * inv
    stats2 = exchange(
        1,
        (
            jnp.sum(d_normed, axis=-1, keepdims=True),
            jnp.sum(d_normed * unit, axis=-1, keepdims=True),
        ),
    )

    for s, d in enumerate((1, -1)):
        gh[(1, d)].wait_recv()
        gh[(2, d)].wait_recv()
    gb_y.wait_recv()
    mine = chip(0, y)
    gw_ref[:half, :] = (
        gown[mine, :half, :].astype(F32) + gxh[2, 0].astype(F32) + gxh[2, 1].astype(F32)
    ).astype(BF16)
    gw_ref[half:, :] = (
        gown[mine, half:, :].astype(F32) + gxh[1, 0].astype(F32) + gxh[1, 1].astype(F32)
        + gyb[...].astype(F32)
    ).astype(BF16)

    for cp in stats2:
        cp.wait_recv()
    sums = rows_to_columns(jnp.sum(stat_in[1], axis=0)) * (1.0 / (16.0 * width))
    gt_ref[...] = inv * (d_normed - sums[:, 0:1] - unit * sums[:, 1:2])

    for cp in started + stats + stats2:
        cp.wait_send()


SENDS = 121


def per_device(tokens, w_qkv, out_grad):
    rows, width = tokens.shape
    depth, cols = w_qkv.shape
    half, quarter = depth // 2, depth // 4
    vmem = pltpu.VMEM
    scratch = [
        vmem((8, 2 * depth, cols), BF16),
        vmem((16, rows, width), BF16),
        vmem((8, rows, 2 * width), BF16),
        vmem((16, width, rows), BF16),
        vmem((rows, cols), F32),
        vmem((rows, cols), BF16),
        vmem((rows, cols), BF16),
        vmem((8, depth, cols), BF16),
        vmem((8, depth, cols), BF16),
        vmem((8, depth, cols), BF16),
        vmem((4, half, cols), BF16),
        vmem((3, 2, quarter, cols), BF16),
        vmem((3, 2, half, cols), BF16),
        vmem((half, cols), BF16),
        vmem((16, rows, width), BF16),
        vmem((2, 2, rows // 2, width), BF16),
        vmem((2, 2, 3, rows, width), BF16),
        vmem((rows, width), BF16),
        vmem((2, 8, rows), F32),
        vmem((2, 16, 8, rows), F32),
        pltpu.SemaphoreType.DMA((SENDS,)),
        pltpu.SemaphoreType.DMA((SENDS,)),
        pltpu.SemaphoreType.DMA((2, 16)),
        pltpu.SemaphoreType.DMA((2, 16)),
    ]
    return pl.pallas_call(
        kernel,
        out_shape=(
            jax.ShapeDtypeStruct(out_grad.shape, BF16),
            jax.ShapeDtypeStruct(tokens.shape, F32),
            jax.ShapeDtypeStruct(w_qkv.shape, BF16),
        ),
        in_specs=[pl.BlockSpec(memory_space=vmem)] * 3,
        out_specs=(pl.BlockSpec(memory_space=vmem),) * 3,
        scratch_shapes=scratch,
        compiler_params=pltpu.CompilerParams(
            collective_id=0, has_side_effects=True, vmem_limit_bytes=62 * 1024 * 1024
        ),
    )(tokens, w_qkv, out_grad)


def solution(mesh):
    placed = (P("dp", "mp"), P("dp", "mp"), P("dp", "mp"))
    return jax.shard_map(
        per_device, mesh=mesh, in_specs=placed, out_specs=placed, check_vma=False
    )
```

time: 472 us -> 122 us (0.26)
  waiting for transfers between devices: 418 us -> 0 us
  Pallas kernels: 0 us -> 116 us
  matrix products: 23.3 us -> 0 us
  between operations: 14 us -> 0.65 us
  other arithmetic: 11.7 us -> 0 us
    all_gather x2 -> x0, waiting for transfers between devices: 152 us -> none  [the longest x1 96 us: per_device(): gathered = lax.all_gather(tokens, 'mp', axis=1, tiled=True)]
    psum x1 -> x0, waiting for transfers between devices: 152 us -> none  [per_device(): lax.psum(back_term.astype(jnp.bfloat16), 'mp').astype(jnp.float32)]
    pallas_call x0 -> x1, Pallas kernels: none -> 116 us  [per_device(): pl.pallas_call(kernel, out_shape=(jax.ShapeDtypeStruct(out_grad.shape, BF...]
    reduce_scatter x1 -> x0, waiting for transfers between devices: 112 us -> none  [per_device(): lax.psum_scatter(lax.dot_general(normed, d_qkv, (((0,), (0,)), ((), ())),...]
    dot_general x9 -> x0, matrix products: 23.3 us -> none  [the longest x1 7.08 us: per_device(): projected = jnp.dot(normed, weights, preferred_element_type=jnp.float32)]
    reduce_sum x6 -> x0, other arithmetic: 7.67 us -> none  [the longest x2 2.93 us: normalize_rows(): jnp.mean(centred * centred, axis=-1, keepdims=True) + 1e-06]
  transfers between devices with their start and end apart: 4 -> 0, of which waited for: 4 -> 0; matrix products, arithmetic and copies ran while one was open for 4% -> 0% of each run, Pallas kernels for 0% -> 0%
where the time goes in v1:
time: 122 us; the launch traced here: 121 us
  Pallas kernels  116 us (95%)
  local copies, waits for them, and re-layouts  4.21 us (3%)
    pallas_call x1, Pallas kernels, per_device(): pl.pallas_call(kernel, out_shape=(jax.ShapeDtypeStruct(out_grad.shape, BF...  116 us
    unnamed x5, local copies, waits for them, and re-layouts  4.21 us

profile of v1, /device:TPU:1, one launch (start us, length us, event | category | flops | bytes accessed | tf_op | source)
XLA Modules:
  0.0 120.8 jit_solution(13177596514224307148)
XLA Ops:
  0.6 116.0 %shard_map.58 = (bf16[256,256]{1,0:T(8,128)(2,1)}, f32[256,384]{1,0:T(8,128)}, bf16[384,768]{1,0:T(8,128)(2,1)}) custom-call(bf16[256,384]{1,0:T(8,128)(2,1)} %tok_ref.1, bf16[384,768]{1,0:T(8,128)(2,1)} %w_ref.1, bf16[256,256]{1,0:T(8,128)(2,1)} %og_ref.1), custom_call_target="tpu_custom_call" | custom-call | tf_op jit(solution)/shard_map/pallas_call | solution.py:432
  116.6 0.0 copy-start
  116.6 1.6 %copy.9 = bf16[256,256]{1,0:T(8,128)(2,1)} copy(bf16[256,256]{1,0:T(8,128)(2,1)} %get-tuple-element.6) | data formatting | bytes 262144
  118.2 1.8 %copy.10 = f32[256,384]{1,0:T(8,128)} copy(f32[256,384]{1,0:T(8,128)} %get-tuple-element.7) | data formatting | bytes 786432
  120.0 0.0 copy-done
  120.0 0.8 copy.11
Async XLA Ops:
  116.6 3.4 %copy-start = (bf16[384,768]{1,0:T(8,128)(2,1)S(1)}, bf16[384,768]{1,0:T(8,128)(2,1)}, u32[]{:S(2)}) copy-start(bf16[384,768]{1,0:T(8,128)(2,1)} %get-tuple-element.8) | copy-start | bytes 1769476

commit v2 on v0

v2 whole, which is shorter than its diff:
```python
import jax
import jax.numpy as jnp
from jax import lax
from jax.experimental import pallas as pl
from jax.experimental.pallas import tpu as pltpu
from jax.sharding import PartitionSpec as P

HD = 128
EPS = 1e-06
F32 = jnp.float32
BF16 = jnp.bfloat16
MESH = pl.DeviceIdType.MESH
SIGN = {"+": 1, "-": -1}
OTHER = {"+": "-", "-": "+"}

ORDER = (
    37, 6, 23, 87, 7, 56, 38, 39, 5, 55,
    8, 21, 57, 22, 24, 1, 2, 0, 25, 40,
    88, 59, 45, 13, 27, 58, 41, 62, 11, 48,
    52, 73, 75, 9, 60, 46, 66, 3, 69, 14,
    29, 30, 42, 63, 35, 15, 53, 77, 79, 49,
    4, 61, 47, 19, 26, 32, 67, 70, 28, 16,
    33, 64, 81, 43, 12, 54, 50, 83, 10, 17,
    31, 68, 71, 85, 89, 136, 144, 108, 36, 134,
    132, 102, 104, 140, 65, 112, 106, 114, 44, 110,
    18, 130, 142, 116, 34, 20, 51, 72, 138, 95,
    92, 93, 97, 91, 90, 94, 96, 98, 179, 105,
    109, 139, 169, 111, 107, 180, 137, 152, 164, 172,
    99, 170, 145, 131, 153, 146, 133, 173, 174, 141,
    147, 115, 177, 135, 143, 167, 175, 189, 154, 178,
    155, 181, 100, 168, 103, 183, 148, 118, 165, 149,
    124, 117, 119, 125, 162, 113, 156, 74, 171, 157,
    76, 163, 182, 150, 151, 120, 184, 176, 121, 191,
    126, 127, 78, 160, 80, 166, 188, 158, 185, 190,
    122, 123, 128, 82, 129, 84, 193, 86, 101, 159,
    161, 186, 192, 187,
)


def mm(a, b, dims, precision=None):
    return lax.dot_general(
        a, b, (dims, ((), ())), preferred_element_type=F32, precision=precision
    )


def normalize(v):
    centred = v - jnp.mean(v, axis=-1, keepdims=True)
    inv = lax.rsqrt(jnp.mean(centred * centred, axis=-1, keepdims=True) + EPS)
    return centred * inv, inv


def normalize_back(d, unit, inv):
    return inv * (
        d
        - jnp.mean(d, axis=-1, keepdims=True)
        - unit * jnp.mean(d * unit, axis=-1, keepdims=True)
    )


def one_head(q, k, v, og):
    qu, qi = normalize(q.astype(F32))
    ku, ki = normalize(k.astype(F32))
    scale = 1.0 / (HD**0.5)
    scores = mm(qu, ku, ((1,), (1,)), lax.Precision.HIGHEST) * scale
    weights = jnp.exp(scores)
    probs = weights / jnp.sum(weights, axis=-1, keepdims=True)
    probs16 = probs.astype(BF16)
    out = mm(probs16, v, ((1,), (0,)))
    dv = mm(probs16, og, ((0,), (0,)))
    dp = mm(og, v, ((1,), (1,)))
    ds = (probs * (dp - jnp.sum(dp * probs, axis=-1, keepdims=True)) * scale).astype(BF16)
    dq = normalize_back(mm(ds, ku.astype(BF16), ((1,), (0,))), qu, qi)
    dk = normalize_back(mm(ds, qu.astype(BF16), ((0,), (0,))), ku, ki)
    return out, dq, dk, dv


def split_rows(depth):
    a = depth * 3 // 8
    ap = depth * 5 // 24
    bp = depth * 7 // 24
    return {
        "A": (0, a),
        "B": (a, depth - a),
        "A+": (0, ap),
        "A-": (ap, a - ap),
        "B+": (a, bp),
        "B-": (a + bp, depth - a - bp),
    }


def kernel(
    tok_hbm, w_hbm, og_hbm,
    att_hbm, gt_hbm, gw_hbm,
    og_ref, att_ref, gt_ref, gw_ref, load_sem, store_sem,
    wfull, tfull, normed, normt, acc, dqkv, cols,
    gown, gout, gin, gya, gaq, gaf, gad, gbq, gbf, gbd, gyb,
    bk, bin, by, st_own, st_peer, st_ring,
    send_sem, recv_sem,
):
    dp, mp = lax.axis_index("dp"), lax.axis_index("mp")
    x, y, c = dp // 4, (dp // 2) % 2, dp % 2
    yh, z = mp // 8, mp % 8
    rows, width = tok_hbm.shape
    depth = w_hbm.shape[0]
    hrow = rows // 2
    part = split_rows(depth)

    def ring(v, d, n):
        return lax.rem(v + d + n, n)

    sib = {"dp": dp + 1 - 2 * c}
    ydev = {"dp": x * 4 + (1 - y) * 2 + c}
    xdev = {s: {"dp": ring(x, d, 4) * 4 + y * 2 + c} for s, d in SIGN.items()}
    zdev = {s: {"mp": yh * 8 + ring(z, d, 8)} for s, d in SIGN.items()}
    yhdev = {"mp": (1 - yh) * 8 + z}

    own_tok = tfull.at[mp]
    own_w = wfull.at[x * 2 + y, pl.ds(pl.multiple_of(c * depth, 16), depth), :]
    loads = [
        pltpu.make_async_copy(src, dst, load_sem.at[i])
        for i, (src, dst) in enumerate(((tok_hbm, own_tok), (w_hbm, own_w), (og_hbm, og_ref)))
    ]
    stores = []

    def store(src, dst):
        cp = pltpu.make_async_copy(src, dst, store_sem.at[len(stores)])
        cp.start()
        stores.append(cp)

    copies = {}
    steps = {}

    def send(name, src, dst, dev):
        n = len(copies)
        cp = pltpu.make_async_remote_copy(
            src_ref=src, dst_ref=dst, send_sem=send_sem.at[n], recv_sem=recv_sem.at[n],
            device_id=dev, device_id_type=MESH,
        )
        cp.start()
        copies[name] = cp

    def wait(*names):
        for name in names:
            copies[name].wait_recv()

    def step(name):
        def keep(f):
            steps[name] = f
        return keep

    ys = {"y": y, "n": 1 - y}

    def wp(xd, yd, rng):
        r = pl.multiple_of(c * depth + rng[0], 16)
        return wfull.at[ring(x, xd, 4) * 2 + ys[yd], pl.ds(r, rng[1]), :]

    def wown(name, rng, dev):
        send(name, w_hbm.at[pl.ds(*rng), :], wp(0, "y", rng), dev)

    def wsend(name, xd, yd, rng, dev):
        send(name, wp(xd, yd, rng), wp(xd, yd, rng), dev)

    @step("iS")
    def _():
        wown("S0y", (0, depth), sib)

    @step("iBy")
    def _():
        wown("By", part["B"], ydev)

    @step("iAy")
    def _():
        wown("Ay", part["A"], ydev)

    @step("fBy")
    def _():
        wait("By")
        for p, s in (("+", "+"), ("-", "-"), ("-", "+"), ("+", "-")):
            wsend("Bo" + p + s, 0, "n", part["B" + p], xdev[s])
        wsend("SBy", 0, "n", part["B"], sib)

    @step("fAy")
    def _():
        wait("Ay")
        wsend("SAy", 0, "n", part["A"], sib)

    def weight_start(k, p, s):
        @step("i" + k + p + s)
        def _():
            wown(k + p + s, part[k + p], xdev[s])

    def weight_steps(s, d):
        o = OTHER[s]

        def a_piece(p):
            @step("fA" + p + s)
            def _():
                wait("A" + p + s)
                if p == s:
                    wsend("Aq" + s, -d, "y", part["A" + s], xdev[s])
                wsend("Ay" + p + s, -d, "y", part["A" + p], ydev)
                wsend("SA" + p + s, -d, "y", part["A" + p], sib)

            @step("fAy" + p + s)
            def _():
                wait("Ay" + p + s)
                wsend("SAy" + p + s, -d, "n", part["A" + p], sib)

        def b_piece(b, yd):
            @step("f" + b + s + s)
            def _():
                wait(b + s + s)
                wsend(b + "q" + s, -d, yd, part["B" + s], xdev[s])

            @step("f" + b + o + s)
            def _():
                wait(b + o + s)
                wsend("S" + b + s, -d, yd, part["B"], sib)

            @step("f" + b + "q" + s)
            def _():
                wait(b + "q" + s)
                wsend("S" + b + "q" + s, -2 * d, yd, part["B" + s], sib)

        a_piece(s)
        a_piece(o)
        b_piece("B", "y")
        b_piece("Bo", "n")

        @step("fAq" + s)
        def _():
            wait("Aq" + s)
            wsend("Ayq" + s, -2 * d, "y", part["A" + s], ydev)
            wsend("SAq" + s, -2 * d, "y", part["A" + s], sib)

        @step("fAyq" + s)
        def _():
            wait("Ayq" + s)
            wsend("SAyq" + s, -2 * d, "n", part["A" + s], sib)

    for s, d in SIGN.items():
        for p in SIGN:
            weight_start("A", p, s)
            weight_start("B", p, s)
        weight_steps(s, d)

    yb = {"o": yh, "p": 1 - yh}

    def feature(r, zd):
        return yb[r] * 8 + ring(z, zd, 8)

    def tp(r, zd, i):
        return tfull.at[feature(r, zd), pl.ds(i * hrow, hrow), :]

    def is_long(i, s):
        return (i == 0) == (s == "+")

    def token_start(i):
        mine = tok_hbm.at[pl.ds(i * hrow, hrow), :]

        @step("iTh%d" % i)
        def _():
            send("Th%d" % i, mine, tp("o", 0, i), yhdev)

        def along(s):
            @step("iT%d%s" % (i, s))
            def _():
                send("To%d0%s" % (i, s), mine, tp("o", 0, i), zdev[s])

        for s in SIGN:
            along(s)

        @step("fTP%d" % i)
        def _():
            wait("Th%d" % i)
            for s in SIGN:
                send("Tp%d0%s" % (i, s), tp("p", 0, i), tp("p", 0, i), zdev[s])

    def token_hop(r, i, h, s, d):
        @step("fT%s%d%d%s" % (r, i, h, s))
        def _():
            wait("T%s%d%d%s" % (r, i, h - 1, s))
            if h < 3 + is_long(i, s):
                src = tp(r, -d * h, i)
                send("T%s%d%d%s" % (r, i, h, s), src, src, zdev[s])

    for i in range(2):
        token_start(i)
        for r in "op":
            for s, d in SIGN.items():
                for h in range(1, 4 + is_long(i, s)):
                    token_hop(r, i, h, s, d)

    def as_rows(parts):
        lane = lax.broadcasted_iota(jnp.int32, (rows, 128), 1)
        tile = jnp.zeros((rows, 128), F32)
        for i, p in enumerate(parts):
            tile = jnp.where(lane == i, p, tile)
        return jnp.transpose(tile)[:8, :]

    def as_columns(parts):
        pad = jnp.zeros((128 - len(parts), rows), F32)
        return jnp.transpose(jnp.concatenate(list(parts) + [pad], axis=0))

    def stat_send(which, name, s):
        send(name, st_ring.at[which, z], st_ring.at[which, z], zdev[s])

    def stat_hop(which, p, h, s, d):
        @step("%sS%d%s" % ("fb"[which], h, s))
        def _():
            wait("%st%d%s" % (p, h - 1, s))
            if h < 3 or (h == 3 and d == 1):
                src = st_ring.at[which, ring(z, -d * h, 8)]
                send("%st%d%s" % (p, h, s), src, src, zdev[s])

    for h in range(1, 5):
        for s, d in SIGN.items():
            if h < 4 or d == 1:
                stat_hop(0, "S", h, s, d)
                stat_hop(1, "R", h, s, d)

    @step("iSt")
    def _():
        loads[0].wait()
        own = own_tok[...].astype(F32)
        mean = jnp.mean(own, axis=-1, keepdims=True)
        dev = own - mean
        st_own[0] = as_rows((mean, jnp.sum(dev * dev, axis=-1, keepdims=True)))
        send("Sth", st_own.at[0], st_peer.at[0], yhdev)

    @step("fSt")
    def _():
        wait("Sth")
        a, b = st_own[0], st_peer[0]
        gap = a[0:1] - b[0:1]
        st_ring[0, z] = jnp.concatenate(
            [
                0.5 * (a[0:1] + b[0:1]),
                a[1:2] + b[1:2] + (0.5 * width) * gap * gap,
                jnp.zeros((6, rows), F32),
            ],
            axis=0,
        )
        for s in SIGN:
            stat_send(0, "St0" + s, s)

    @step("stat")
    def _():
        got = st_ring[0]
        means = got[:, 0:1, :]
        mean = jnp.mean(means, axis=0)
        gap = means - mean[None]
        sq = jnp.sum(got[:, 1:2, :], axis=0) + (2.0 * width) * jnp.sum(gap * gap, axis=0)
        cols[0] = as_columns((mean, lax.rsqrt(sq / (16.0 * width) + EPS)))
        normed[:, rows:, :] = jnp.ones_like(normed[:, rows:, :])
        acc[...] = jnp.zeros_like(acc)

    def norm_block(r, zd):
        @step("n%s%d" % (r, zd))
        def _():
            j = feature(r, zd)
            unit = (tfull[j].astype(F32) - cols[0, :, 0:1]) * cols[0, :, 1:2]
            unit = unit.astype(BF16)
            lanes = pl.ds(pl.multiple_of((j % 2) * width, 128), width)
            normed[j // 2, :rows, lanes] = unit
            normt[j] = jnp.transpose(unit)

    def product(xd, yd, waits):
        @step("m%d%s" % (xd, yd))
        def _():
            wait(*waits)
            if (xd, yd) == (0, "y"):
                loads[1].wait()
            k = ring(x, xd, 4) * 2 + ys[yd]
            acc[...] += mm(normed[k], wfull[k], ((1,), (0,)))

    product(0, "y", ("S0y",))
    product(0, "n", ("SBy", "SAy"))
    for s, d in SIGN.items():
        product(-d, "y", ("SA+" + s, "SA-" + s, "SB" + s))
        product(-d, "n", ("SAy+" + s, "SAy-" + s, "SBo" + s))
    product(2, "y", ("SAq+", "SAq-", "SBq+", "SBq-"))
    product(2, "n", ("SAyq+", "SAyq-", "SBoq+", "SBoq-"))

    @step("att")
    def _():
        loads[2].wait()
        for h in range(2):
            base = 3 * h * HD
            at = [slice(base + i * HD, base + (i + 1) * HD) for i in range(3)]
            qkv = [acc[:rows, a].astype(BF16) for a in at]
            mine = slice(h * HD, (h + 1) * HD)
            out, dq, dk, dv = one_head(*qkv, og_ref[:, mine])
            att_ref[:, mine] = out.astype(BF16)
            for a, g in zip(at, (dq, dk, dv)):
                dqkv[:, a] = g.astype(BF16)
        store(att_ref, att_hbm)

    @step("bSt")
    def _():
        d = dqkv[...].astype(F32)
        st_own[1] = as_rows(
            (
                jnp.sum(d * acc[rows : rows + 1, :], axis=-1, keepdims=True),
                jnp.sum(d * acc[:rows, :], axis=-1, keepdims=True),
            )
        )
        send("Rth", st_own.at[1], st_peer.at[1], yhdev)

    @step("bSh")
    def _():
        wait("Rth")
        st_ring[1, z] = st_own[1] + st_peer[1]
        for s in SIGN:
            stat_send(1, "Rt0" + s, s)

    @step("bstat")
    def _():
        sums = jnp.sum(st_ring[1], axis=0) * (1.0 / (16.0 * width))
        cols[1] = as_columns((sums[0:1], sums[1:2]))

    def bp(r, zd, i):
        return bk.at[feature(r, zd), pl.ds(i * hrow, hrow), :]

    def add(dst, *srcs):
        total = dst[...].astype(F32)
        for src in srcs:
            total = total + src[...].astype(F32)
        dst[...] = total.astype(BF16)

    def back(r, zd):
        @step("c%s%d" % (r, zd))
        def _():
            j = feature(r, zd)
            w = wfull[j // 2, pl.ds(pl.multiple_of((j % 2) * depth, 16), depth), :]
            bk[j] = mm(dqkv[...], w, ((1,), (1,))).astype(BF16)
            if zd == 4:
                back_send(r, 0, 0, "+", 4)
                back_send(r, 1, 0, "-", 4)

    def back_send(r, i, h, s, zd):
        dst = bin.at["op".index(r), i, "+-".index(s), h]
        send("K%s%d%d%s" % (r, i, h, s), bp(r, zd, i), dst, zdev[s])

    def got(r, i, h, s):
        return bin.at["op".index(r), i, "+-".index(s), h]

    def back_hop(r, i, h, s, d):
        @step("k%s%d%d%s" % (r, i, h, s))
        def _():
            zd = d * (4 - h)
            if h > 1 or is_long(i, s):
                wait("K%s%d%d%s" % (r, i, h - 1, s))
                add(bp(r, zd, i), got(r, i, h - 1, s))
            back_send(r, i, h, s, zd)

    for r in "op":
        for zd in (0, 1, 2, 3, 4, -1, -2, -3):
            norm_block(r, zd)
            back(r, zd)
        for i in range(2):
            for h in (1, 2, 3):
                for s, d in SIGN.items():
                    back_hop(r, i, h, s, d)

    def back_end(i):
        mine = pl.ds(i * hrow, hrow)

        @step("kp%d" % i)
        def _():
            wait("Kp%d3+" % i, "Kp%d3-" % i)
            add(bp("p", 0, i), got("p", i, 3, "+"), got("p", i, 3, "-"))
            send("Kh%d" % i, bp("p", 0, i), by.at[mine, :], yhdev)

        @step("ft%d" % i)
        def _():
            wait("Ko%d3+" % i, "Ko%d3-" % i, "Kh%d" % i)
            total = bp("o", 0, i)[...].astype(F32) + by[mine, :].astype(F32)
            for s in SIGN:
                total = total + got("o", i, 3, s)[...].astype(F32)
            mean, inv = cols[0, mine, 0:1], cols[0, mine, 1:2]
            unit = (tp("o", 0, i)[...].astype(F32) - mean) * inv
            gt_ref[mine, :] = inv * (total - cols[1, mine, 0:1] - unit * cols[1, mine, 1:2])
            store(gt_ref.at[mine, :], gt_hbm.at[mine, :])

    back_end(0)
    back_end(1)

    def chip(xd, yd):
        return ring(x, xd, 4) * 2 + ys[yd]

    def gp(xd, yd, rng):
        return gown.at[chip(xd, yd), pl.ds(*rng), :]

    XS = (0, 1, -1, 2)
    TOWARD = {1: "+", -1: "-"}

    def grad(xd, yd):
        @step("g%d%s" % (xd, yd))
        def _():
            q = chip(xd, yd)
            gout[q] = mm(normt[2 * q + 1 - c], dqkv[...], ((1,), (0,))).astype(BF16)
            send("G%d%s" % (xd, yd), gout.at[q], gin.at[q], sib)
            gown[q] = mm(normt[2 * q + c], dqkv[...], ((1,), (0,))).astype(BF16)

        @step("j%d%s" % (xd, yd))
        def _():
            wait("G%d%s" % (xd, yd))
            q = chip(xd, yd)
            add(gown.at[q], gin.at[q])
            if yd == "n":
                send("Y%d" % xd, gp(xd, "n", part["A"]), gya.at[XS.index(xd)], ydev)
            yi = "yn".index(yd)
            if xd == 2:
                for s in SIGN:
                    send("BQ" + yd + s, gp(2, yd, part["B" + s]), gbq[s].at[yi], xdev[s])
            elif xd != 0:
                s = TOWARD[xd]
                p = OTHER[s]
                send("BF" + yd + s, gp(xd, yd, part["B" + p]), gbf[p].at[yi], xdev[s])

    def sum_y(xd):
        @step("ya%d" % xd)
        def _():
            wait("Y%d" % xd)
            add(gp(xd, "y", part["A"]), gya.at[XS.index(xd)])
            if xd == 2:
                for s in SIGN:
                    send("AQ" + s, gp(2, "y", part["A" + s]), gaq[s], xdev[s])
            elif xd != 0:
                s = TOWARD[xd]
                p = OTHER[s]
                send("AF" + s, gp(xd, "y", part["A" + p]), gaf[p], xdev[s])

    def sum_x(s, d):
        def along(yd):
            yi = "yn".index(yd)

            @step("bh" + yd + s)
            def _():
                wait("BQ" + yd + s)
                add(gp(d, yd, part["B" + s]), gbq[s].at[yi])
                send("BD" + yd + s, gp(d, yd, part["B" + s]), gbd[s].at[yi], xdev[s])

        along("y")
        along("n")

        @step("ah" + s)
        def _():
            wait("AQ" + s)
            add(gp(d, "y", part["A" + s]), gaq[s])
            send("AD" + s, gp(d, "y", part["A" + s]), gad[s], xdev[s])

        @step("bn" + s)
        def _():
            wait("BDn" + s, "BFn" + OTHER[s])
            add(gp(0, "n", part["B" + s]), gbd[s].at[1], gbf[s].at[1])
            send("Yb" + s, gp(0, "n", part["B" + s]), gyb[s], ydev)

        def finish(rng, *terms):
            total = gp(0, "y", rng)[...].astype(F32)
            for t in terms:
                total = total + t[...].astype(F32)
            mine = pl.ds(*rng)
            gw_ref[mine, :] = total.astype(BF16)
            store(gw_ref.at[mine, :], gw_hbm.at[mine, :])

        @step("fgA" + s)
        def _():
            wait("AD" + s, "AF" + OTHER[s])
            finish(part["A" + s], gad[s], gaf[s])

        @step("fgB" + s)
        def _():
            wait("BDy" + s, "BFy" + OTHER[s], "Yb" + s)
            finish(part["B" + s], gbd[s].at[0], gbf[s].at[0], gyb[s])

    for xd in XS:
        grad(xd, "y")
        grad(xd, "n")
        sum_y(xd)
    for s, d in SIGN.items():
        sum_x(s, d)

    for cp in loads:
        cp.start()
    barrier = pltpu.get_barrier_semaphore()
    everyone = [sib, ydev, xdev["+"], xdev["-"], zdev["+"], zdev["-"], yhdev]
    for dev in everyone:
        pl.semaphore_signal(barrier, inc=1, device_id=dev, device_id_type=MESH)
    pl.semaphore_wait(barrier, len(everyone))

    todo = list(steps.values())
    assert sorted(ORDER) == list(range(len(todo)))
    for n in ORDER:
        todo[n]()
    assert len(copies) == COPIES
    for cp in copies.values():
        cp.wait_send()
    for cp in stores:
        cp.wait()


COPIES = 157


def hand_over(*refs):
    for src, dst in zip(refs[:3], refs[3:]):
        dst[...] = src[...]


def per_device(tokens, w_qkv, out_grad):
    rows, width = tokens.shape
    depth, wide = w_qkv.shape
    part = split_rows(depth)
    vmem = pltpu.VMEM

    def count(name):
        return part[name][1]

    a_part = {s: vmem((count("A" + s), wide), BF16) for s in SIGN}
    b_part = {s: vmem((count("B" + s), wide), BF16) for s in SIGN}
    b_pair = {s: vmem((2, count("B" + s), wide), BF16) for s in SIGN}
    scratch = [
        vmem(out_grad.shape, BF16),
        vmem(out_grad.shape, BF16),
        vmem(tokens.shape, F32),
        vmem(w_qkv.shape, BF16),
        pltpu.SemaphoreType.DMA((3,)),
        pltpu.SemaphoreType.DMA((7,)),
        vmem((8, 2 * depth, wide), BF16),
        vmem((16, rows, width), BF16),
        vmem((8, rows + 16, 2 * width), BF16),
        vmem((16, width, rows), BF16),
        vmem((rows + 16, wide), F32),
        vmem((rows, wide), BF16),
        vmem((2, rows, 128), F32),
        vmem((8, depth, wide), BF16),
        vmem((8, depth, wide), BF16),
        vmem((8, depth, wide), BF16),
        vmem((4, count("A"), wide), BF16),
        a_part, a_part, a_part, b_pair, b_pair, b_pair, b_part,
        vmem((16, rows, width), BF16),
        vmem((2, 2, 2, 4, rows // 2, width), BF16),
        vmem((rows, width), BF16),
        vmem((2, 8, rows), F32),
        vmem((2, 8, rows), F32),
        vmem((2, 8, 8, rows), F32),
        pltpu.SemaphoreType.DMA((COPIES,)),
        pltpu.SemaphoreType.DMA((COPIES,)),
    ]
    anywhere = pl.BlockSpec(memory_space=pl.ANY)
    results = pl.pallas_call(
        kernel,
        out_shape=(
            jax.ShapeDtypeStruct(out_grad.shape, BF16),
            jax.ShapeDtypeStruct(tokens.shape, F32),
            jax.ShapeDtypeStruct(w_qkv.shape, BF16),
        ),
        in_specs=[anywhere] * 3,
        out_specs=(anywhere,) * 3,
        scratch_shapes=scratch,
        compiler_params=pltpu.CompilerParams(
            collective_id=0, has_side_effects=True, vmem_limit_bytes=62 * 1024 * 1024
        ),
    )(tokens, w_qkv, out_grad)
    in_vmem = [pl.BlockSpec(memory_space=vmem)] * 3
    return pl.pallas_call(
        hand_over,
        out_shape=[jax.ShapeDtypeStruct(r.shape, r.dtype) for r in results],
        in_specs=in_vmem,
        out_specs=in_vmem,
    )(*results)


def solution(mesh):
    placed = (P("dp", "mp"), P("dp", "mp"), P("dp", "mp"))
    return jax.shard_map(
        per_device, mesh=mesh, in_specs=placed, out_specs=placed, check_vma=False
    )
```

time: 472 us -> 93.4 us (0.20)
  waiting for transfers between devices: 418 us -> 0 us
  Pallas kernels: 0 us -> 92.7 us
  matrix products: 23.3 us -> 0 us
  between operations: 14 us -> 0.64 us
  other arithmetic: 11.7 us -> 0 us
    all_gather x2 -> x0, waiting for transfers between devices: 152 us -> none  [the longest x1 96 us: per_device(): gathered = lax.all_gather(tokens, 'mp', axis=1, tiled=True)]
    psum x1 -> x0, waiting for transfers between devices: 152 us -> none  [per_device(): lax.psum(back_term.astype(jnp.bfloat16), 'mp').astype(jnp.float32)]
    reduce_scatter x1 -> x0, waiting for transfers between devices: 112 us -> none  [per_device(): lax.psum_scatter(lax.dot_general(normed, d_qkv, (((0,), (0,)), ((), ())),...]
    pallas_call x0 -> x2, Pallas kernels: none -> 92.7 us  [the longest x1 90.4 us: per_device(): pl.pallas_call(kernel, out_shape=(jax.ShapeDtypeStruct(out_grad.shape, BF...]
    dot_general x9 -> x0, matrix products: 23.3 us -> none  [the longest x1 7.08 us: per_device(): projected = jnp.dot(normed, weights, preferred_element_type=jnp.float32)]
    reduce_sum x6 -> x0, other arithmetic: 7.67 us -> none  [the longest x2 2.93 us: normalize_rows(): jnp.mean(centred * centred, axis=-1, keepdims=True) + 1e-06]
  transfers between devices with their start and end apart: 4 -> 0, of which waited for: 4 -> 0; matrix products, arithmetic and copies ran while one was open for 4% -> 0% of each run, Pallas kernels for 0% -> 0%
where the time goes in v2:
time: 93.4 us; the launch traced here: 93.3 us
  Pallas kernels  92.7 us (99%)
    pallas_call x1, Pallas kernels, per_device(): pl.pallas_call(kernel, out_shape=(jax.ShapeDtypeStruct(out_grad.shape, BF...  90.4 us
    pallas_call x1, Pallas kernels, per_device(): pl.pallas_call(hand_over, out_shape=[jax.ShapeDtypeStruct(r.shape, r.dtyp...  2.26 us

profile of v2, /device:TPU:1, one launch (start us, length us, event | category | flops | bytes accessed | tf_op | source)
XLA Modules:
  0.0 93.3 jit_solution(2939736570910112305)
XLA Ops:
  0.6 90.4 %shard_map.58 = (bf16[256,256]{1,0:T(8,128)(2,1)}, f32[256,384]{1,0:T(8,128)}, bf16[384,768]{1,0:T(8,128)(2,1)}) custom-call(bf16[256,384]{1,0:T(8,128)(2,1)} %tok_hbm.1, bf16[384,768]{1,0:T(8,128)(2,1)} %w_hbm.1, bf16[256,256]{1,0:T(8,128)(2,1)} %og_hbm.1), custom_call_target="tpu_custom_call" | custom-call | tf_op jit(solution)/shard_map/pallas_call | solution.py:653
  91.0 2.3 %shard_map.59 = (bf16[256,256]{1,0:T(8,128)(2,1)}, f32[256,384]{1,0:T(8,128)}, bf16[384,768]{1,0:T(8,128)(2,1)}) custom-call(bf16[256,256]{1,0:T(8,128)(2,1)} %get-tuple-element.6.refs_0_, f32[256,384]{1,0:T(8,128)} %get-tuple-element.7.refs_1_, bf16[384,768]{1,0:T(8,128)(2,1)} %get-tuple-element.8.refs_2_), custom_call_target="tpu_custom_call" | custom-call | tf_op jit(solution)/shard_map/pallas_call | solution.py:668

commit v3 on v2

--- a/solution.py
+++ b/solution.py
@@ -14,33 +14,33 @@
 OTHER = {"+": "-", "-": "+"}
 
 ORDER = (
-    37, 6, 23, 87, 7, 56, 38, 39, 5, 55,
-    8, 21, 57, 22, 24, 1, 2, 0, 25, 40,
-    88, 59, 45, 13, 27, 58, 41, 62, 11, 48,
-    52, 73, 75, 9, 60, 46, 66, 3, 69, 14,
-    29, 30, 42, 63, 35, 15, 53, 77, 79, 49,
-    4, 61, 47, 19, 26, 32, 67, 70, 28, 16,
-    33, 64, 81, 43, 12, 54, 50, 83, 10, 17,
-    31, 68, 71, 85, 89, 136, 144, 108, 36, 134,
-    132, 102, 104, 140, 65, 112, 106, 114, 44, 110,
-    18, 130, 142, 116, 34, 20, 51, 72, 138, 95,
-    92, 93, 97, 91, 90, 94, 96, 98, 179, 105,
-    109, 139, 169, 111, 107, 180, 137, 152, 164, 172,
-    99, 170, 145, 131, 153, 146, 133, 173, 174, 141,
-    147, 115, 177, 135, 143, 167, 175, 189, 154, 178,
-    155, 181, 100, 168, 103, 183, 148, 118, 165, 149,
-    124, 117, 119, 125, 162, 113, 156, 74, 171, 157,
-    76, 163, 182, 150, 151, 120, 184, 176, 121, 191,
-    126, 127, 78, 160, 80, 166, 188, 158, 185, 190,
-    122, 123, 128, 82, 129, 84, 193, 86, 101, 159,
-    161, 186, 192, 187,
+    39, 57, 38, 5, 24, 21, 87, 37, 55, 1,
+    56, 7, 22, 8, 23, 0, 2, 6, 45, 41,
+    88, 9, 62, 59, 29, 40, 11, 46, 42, 75,
+    73, 58, 27, 63, 60, 30, 52, 48, 13, 14,
+    25, 47, 43, 79, 77, 3, 69, 19, 66, 31,
+    64, 61, 4, 15, 35, 53, 49, 83, 10, 44,
+    70, 81, 16, 12, 32, 65, 67, 28, 54, 50,
+    85, 89, 113, 143, 125, 149, 139, 123, 17, 151,
+    71, 121, 145, 33, 115, 68, 153, 26, 141, 117,
+    111, 92, 94, 20, 100, 96, 51, 34, 90, 102,
+    18, 98, 36, 119, 72, 147, 101, 97, 95, 99,
+    91, 93, 103, 104, 105, 106, 195, 196, 107, 148,
+    203, 197, 202, 181, 154, 124, 200, 199, 182, 144,
+    146, 204, 161, 142, 156, 189, 108, 183, 201, 188,
+    155, 162, 174, 175, 120, 152, 192, 150, 185, 122,
+    193, 190, 207, 112, 158, 176, 205, 194, 178, 179,
+    140, 109, 172, 157, 116, 164, 186, 198, 171, 114,
+    180, 187, 163, 213, 118, 133, 74, 127, 126, 173,
+    134, 128, 184, 160, 159, 76, 165, 166, 212, 209,
+    191, 214, 135, 136, 78, 206, 130, 129, 208, 177,
+    167, 80, 169, 215, 137, 138, 82, 132, 131, 84,
+    211, 86, 110, 170, 210, 168, 217, 216,
 )
 
 
-def mm(a, b, dims, precision=None):
-    return lax.dot_general(
-        a, b, (dims, ((), ())), preferred_element_type=F32, precision=precision
-    )
+def mm(a, b, dims):
+    return lax.dot_general(a, b, (dims, ((), ())), preferred_element_type=F32)
 
 
 def normalize(v):
@@ -57,11 +57,17 @@
     )
 
 
+def split(v, which):
+    high = v.astype(BF16)
+    low = (v - high.astype(F32)).astype(BF16)
+    return jnp.concatenate((high, high, low) if which else (high, low, high), axis=1)
+
+
 def one_head(q, k, v, og):
     qu, qi = normalize(q.astype(F32))
     ku, ki = normalize(k.astype(F32))
     scale = 1.0 / (HD**0.5)
-    scores = mm(qu, ku, ((1,), (1,)), lax.Precision.HIGHEST) * scale
+    scores = mm(split(qu, 0), split(ku, 1), ((1,), (1,))) * scale
     weights = jnp.exp(scores)
     probs = weights / jnp.sum(weights, axis=-1, keepdims=True)
     probs16 = probs.astype(BF16)
@@ -365,6 +371,11 @@
             normed[j // 2, :rows, lanes] = unit
             normt[j] = jnp.transpose(unit)
 
+    last = (ring(z, 4, 8)) // 2
+
+    def multiply(k):
+        acc[...] += mm(normed[k], wfull[k], ((1,), (0,)))
+
     def product(xd, yd, waits):
         @step("m%d%s" % (xd, yd))
         def _():
@@ -372,7 +383,18 @@
             if (xd, yd) == (0, "y"):
                 loads[1].wait()
             k = ring(x, xd, 4) * 2 + ys[yd]
-            acc[...] += mm(normed[k], wfull[k], ((1,), (0,)))
+
+            @pl.when(lax.rem(k, 4) != last)
+            def _():
+                multiply(k)
+
+        @step("l%d%s" % (xd, yd))
+        def _():
+            k = ring(x, xd, 4) * 2 + ys[yd]
+
+            @pl.when(lax.rem(k, 4) == last)
+            def _():
+                multiply(k)
 
     product(0, "y", ("S0y",))
     product(0, "n", ("SBy", "SAy"))
@@ -382,10 +404,11 @@
     product(2, "y", ("SAq+", "SAq-", "SBq+", "SBq-"))
     product(2, "n", ("SAyq+", "SAyq-", "SBoq+", "SBoq-"))
 
-    @step("att")
-    def _():
-        loads[2].wait()
-        for h in range(2):
+    def head(h):
+        @step("att%d" % h)
+        def _():
+            if h == 0:
+                loads[2].wait()
             base = 3 * h * HD
             at = [slice(base + i * HD, base + (i + 1) * HD) for i in range(3)]
             qkv = [acc[:rows, a].astype(BF16) for a in at]
@@ -394,7 +417,11 @@
             att_ref[:, mine] = out.astype(BF16)
             for a, g in zip(at, (dq, dk, dv)):
                 dqkv[:, a] = g.astype(BF16)
-        store(att_ref, att_hbm)
+            if h == 1:
+                store(att_ref, att_hbm)
+
+    head(0)
+    head(1)
 
     @step("bSt")
     def _():
@@ -489,44 +516,62 @@
     def chip(xd, yd):
         return ring(x, xd, 4) * 2 + ys[yd]
 
-    def gp(xd, yd, rng):
-        return gown.at[chip(xd, yd), pl.ds(*rng), :]
+    def gp(xd, yd, rng, lanes=slice(None)):
+        return gown.at[chip(xd, yd), pl.ds(*rng), lanes]
 
     XS = (0, 1, -1, 2)
     TOWARD = {1: "+", -1: "-"}
 
-    def grad(xd, yd):
-        @step("g%d%s" % (xd, yd))
-        def _():
-            q = chip(xd, yd)
-            gout[q] = mm(normt[2 * q + 1 - c], dqkv[...], ((1,), (0,))).astype(BF16)
-            send("G%d%s" % (xd, yd), gout.at[q], gin.at[q], sib)
-            gown[q] = mm(normt[2 * q + c], dqkv[...], ((1,), (0,))).astype(BF16)
-
-        @step("j%d%s" % (xd, yd))
-        def _():
-            wait("G%d%s" % (xd, yd))
-            q = chip(xd, yd)
-            add(gown.at[q], gin.at[q])
+    def part_name(h):
+        return "" if h is None else str(h)
+
+    def grad(xd, yd, h=None):
+        lanes = slice(None) if h is None else pl.ds(h * 3 * HD, 3 * HD)
+        name = "%d%s%s" % (xd, yd, part_name(h))
+        yi = "yn".index(yd)
+
+        def block(ref):
+            return ref.at[chip(xd, yd), :, lanes]
+
+        @step("g" + name)
+        def _():
+            out = block(gout)
+            out[...] = mm(normt[2 * chip(xd, yd) + 1 - c], dqkv[:, lanes], ((1,), (0,))).astype(BF16)
+            send("G" + name, out, block(gin), sib)
+
+        @step("o" + name)
+        def _():
+            mine = mm(normt[2 * chip(xd, yd) + c], dqkv[:, lanes], ((1,), (0,)))
+            block(gown)[...] = mine.astype(BF16)
+
+        @step("j" + name)
+        def _():
+            wait("G" + name)
+            add(block(gown), block(gin))
             if yd == "n":
-                send("Y%d" % xd, gp(xd, "n", part["A"]), gya.at[XS.index(xd)], ydev)
-            yi = "yn".index(yd)
+                dst = gya.at[XS.index(xd), :, lanes]
+                send("Y%d%s" % (xd, part_name(h)), gp(xd, "n", part["A"], lanes), dst, ydev)
             if xd == 2:
                 for s in SIGN:
-                    send("BQ" + yd + s, gp(2, yd, part["B" + s]), gbq[s].at[yi], xdev[s])
+                    dst = gbq[s].at[yi, :, lanes]
+                    send("BQ" + yd + s + part_name(h), gp(2, yd, part["B" + s], lanes), dst, xdev[s])
             elif xd != 0:
                 s = TOWARD[xd]
                 p = OTHER[s]
                 send("BF" + yd + s, gp(xd, yd, part["B" + p]), gbf[p].at[yi], xdev[s])
 
-    def sum_y(xd):
-        @step("ya%d" % xd)
-        def _():
-            wait("Y%d" % xd)
-            add(gp(xd, "y", part["A"]), gya.at[XS.index(xd)])
+    def sum_y(xd, h=None):
+        lanes = slice(None) if h is None else pl.ds(h * 3 * HD, 3 * HD)
+        name = "%d%s" % (xd, part_name(h))
+
+        @step("ya" + name)
+        def _():
+            wait("Y" + name)
+            add(gp(xd, "y", part["A"], lanes), gya.at[XS.index(xd), :, lanes])
             if xd == 2:
                 for s in SIGN:
-                    send("AQ" + s, gp(2, "y", part["A" + s]), gaq[s], xdev[s])
+                    dst = gaq[s].at[:, lanes]
+                    send("AQ" + s + part_name(h), gp(2, "y", part["A" + s], lanes), dst, xdev[s])
             elif xd != 0:
                 s = TOWARD[xd]
                 p = OTHER[s]
@@ -538,7 +583,7 @@
 
             @step("bh" + yd + s)
             def _():
-                wait("BQ" + yd + s)
+                wait("BQ" + yd + s + "0", "BQ" + yd + s + "1")
                 add(gp(d, yd, part["B" + s]), gbq[s].at[yi])
                 send("BD" + yd + s, gp(d, yd, part["B" + s]), gbd[s].at[yi], xdev[s])
 
@@ -547,7 +592,7 @@
 
         @step("ah" + s)
         def _():
-            wait("AQ" + s)
+            wait("AQ" + s + "0", "AQ" + s + "1")
             add(gp(d, "y", part["A" + s]), gaq[s])
             send("AD" + s, gp(d, "y", part["A" + s]), gad[s], xdev[s])
 
@@ -576,9 +621,10 @@
             finish(part["B" + s], gbd[s].at[0], gbf[s].at[0], gyb[s])
 
     for xd in XS:
-        grad(xd, "y")
-        grad(xd, "n")
-        sum_y(xd)
+        for h in (0, 1) if xd == 2 else (None,):
+            grad(xd, "y", h)
+            grad(xd, "n", h)
+            sum_y(xd, h)
     for s, d in SIGN.items():
         sum_x(s, d)
 
@@ -601,7 +647,7 @@
         cp.wait()
 
 
-COPIES = 157
+COPIES = 166
 
 
 def hand_over(*refs):

time: 93.4 us -> 90.7 us (0.971)
  Pallas kernels: 92.7 us -> 90 us
    pallas_call x1, Pallas kernels: 90.4 us -> 87.7 us  [per_device(): pl.pallas_call(kernel, out_shape=(jax.ShapeDtypeStruct(out_grad.shape, BF...]
where the time goes in v3:
time: 90.7 us; the launch traced here: 90.6 us
  Pallas kernels  90 us (99%)
    pallas_call x1, Pallas kernels, per_device(): pl.pallas_call(kernel, out_shape=(jax.ShapeDtypeStruct(out_grad.shape, BF...  87.7 us
    pallas_call x1, Pallas kernels, per_device(): pl.pallas_call(hand_over, out_shape=[jax.ShapeDtypeStruct(r.shape, r.dtyp...  2.26 us

profile of v3, /device:TPU:1, one launch (start us, length us, event | category | flops | bytes accessed | tf_op | source)
XLA Modules:
  0.0 90.6 jit_solution(1296785108480308383)
XLA Ops:
  0.6 87.7 %shard_map.58 = (bf16[256,256]{1,0:T(8,128)(2,1)}, f32[256,384]{1,0:T(8,128)}, bf16[384,768]{1,0:T(8,128)(2,1)}) custom-call(bf16[256,384]{1,0:T(8,128)(2,1)} %tok_hbm.1, bf16[384,768]{1,0:T(8,128)(2,1)} %w_hbm.1, bf16[256,256]{1,0:T(8,128)(2,1)} %og_hbm.1), custom_call_target="tpu_custom_call" | custom-call | tf_op jit(solution)/shard_map/pallas_call | solution.py:699
  88.4 2.3 %shard_map.59 = (bf16[256,256]{1,0:T(8,128)(2,1)}, f32[256,384]{1,0:T(8,128)}, bf16[384,768]{1,0:T(8,128)(2,1)}) custom-call(bf16[256,256]{1,0:T(8,128)(2,1)} %get-tuple-element.6.refs_0_, f32[256,384]{1,0:T(8,128)} %get-tuple-element.7.refs_1_, bf16[384,768]{1,0:T(8,128)(2,1)} %get-tuple-element.8.refs_2_), custom_call_target="tpu_custom_call" | custom-call | tf_op jit(solution)/shard_map/pallas_call | solution.py:714

commit v4 on v3

--- a/solution.py
+++ b/solution.py
@@ -14,28 +14,27 @@
 OTHER = {"+": "-", "-": "+"}
 
 ORDER = (
-    39, 57, 38, 5, 24, 21, 87, 37, 55, 1,
-    56, 7, 22, 8, 23, 0, 2, 6, 45, 41,
-    88, 9, 62, 59, 29, 40, 11, 46, 42, 75,
-    73, 58, 27, 63, 60, 30, 52, 48, 13, 14,
-    25, 47, 43, 79, 77, 3, 69, 19, 66, 31,
-    64, 61, 4, 15, 35, 53, 49, 83, 10, 44,
-    70, 81, 16, 12, 32, 65, 67, 28, 54, 50,
-    85, 89, 113, 143, 125, 149, 139, 123, 17, 151,
-    71, 121, 145, 33, 115, 68, 153, 26, 141, 117,
-    111, 92, 94, 20, 100, 96, 51, 34, 90, 102,
-    18, 98, 36, 119, 72, 147, 101, 97, 95, 99,
-    91, 93, 103, 104, 105, 106, 195, 196, 107, 148,
-    203, 197, 202, 181, 154, 124, 200, 199, 182, 144,
-    146, 204, 161, 142, 156, 189, 108, 183, 201, 188,
-    155, 162, 174, 175, 120, 152, 192, 150, 185, 122,
-    193, 190, 207, 112, 158, 176, 205, 194, 178, 179,
-    140, 109, 172, 157, 116, 164, 186, 198, 171, 114,
-    180, 187, 163, 213, 118, 133, 74, 127, 126, 173,
-    134, 128, 184, 160, 159, 76, 165, 166, 212, 209,
-    191, 214, 135, 136, 78, 206, 130, 129, 208, 177,
-    167, 80, 169, 215, 137, 138, 82, 132, 131, 84,
-    211, 86, 110, 170, 210, 168, 217, 216,
+    87, 23, 7, 55, 37, 5, 1, 39, 56, 21,
+    24, 38, 57, 6, 8, 22, 0, 2, 88, 25,
+    11, 45, 59, 58, 62, 27, 75, 9, 73, 40,
+    41, 46, 60, 13, 29, 69, 66, 77, 63, 79,
+    48, 3, 30, 14, 52, 42, 35, 19, 47, 61,
+    4, 70, 67, 81, 31, 15, 26, 64, 83, 49,
+    12, 53, 43, 16, 32, 28, 71, 68, 85, 89,
+    143, 115, 141, 117, 105, 103, 133, 113, 135, 131,
+    33, 17, 50, 145, 10, 107, 65, 109, 36, 54,
+    137, 90, 91, 92, 93, 94, 18, 44, 111, 72,
+    34, 20, 51, 139, 96, 95, 97, 98, 187, 188,
+    99, 191, 178, 140, 189, 195, 194, 146, 148, 104,
+    170, 112, 171, 180, 100, 196, 164, 181, 134, 172,
+    138, 153, 142, 192, 182, 154, 147, 193, 174, 106,
+    167, 132, 173, 177, 116, 101, 184, 136, 166, 118,
+    120, 205, 114, 175, 199, 197, 185, 155, 126, 179,
+    163, 186, 190, 144, 150, 168, 108, 149, 156, 74,
+    76, 110, 119, 125, 165, 183, 122, 157, 128, 151,
+    78, 176, 207, 152, 121, 158, 80, 127, 201, 169,
+    124, 130, 198, 204, 82, 206, 200, 159, 123, 161,
+    84, 129, 86, 102, 203, 209, 160, 202, 208, 162,
 )
 
 
@@ -81,9 +80,9 @@
 
 
 def split_rows(depth):
-    a = depth * 3 // 8
-    ap = depth * 5 // 24
-    bp = depth * 7 // 24
+    a = depth // 3
+    ap = depth // 6
+    bp = depth // 3
     return {
         "A": (0, a),
         "B": (a, depth - a),
@@ -371,38 +370,41 @@
             normed[j // 2, :rows, lanes] = unit
             normt[j] = jnp.transpose(unit)
 
-    last = (ring(z, 4, 8)) // 2
-
-    def multiply(k):
-        acc[...] += mm(normed[k], wfull[k], ((1,), (0,)))
-
-    def product(xd, yd, waits):
-        @step("m%d%s" % (xd, yd))
-        def _():
-            wait(*waits)
-            if (xd, yd) == (0, "y"):
-                loads[1].wait()
-            k = ring(x, xd, 4) * 2 + ys[yd]
-
-            @pl.when(lax.rem(k, 4) != last)
-            def _():
-                multiply(k)
-
-        @step("l%d%s" % (xd, yd))
-        def _():
-            k = ring(x, xd, 4) * 2 + ys[yd]
-
-            @pl.when(lax.rem(k, 4) == last)
-            def _():
-                multiply(k)
-
-    product(0, "y", ("S0y",))
-    product(0, "n", ("SBy", "SAy"))
+    far = ring(z, 4, 8) // 2
+    same_x, same_y = far // 2 == lax.rem(x, 2), lax.rem(far, 2) == y
+
+    def pick(*four):
+        a, b, c_, d_ = [ring(x, xd, 4) * 2 + ys[yd] for xd, yd in four]
+        return jnp.where(same_y, jnp.where(same_x, a, b), jnp.where(same_x, c_, d_))
+
+    def product(name, k, *chips):
+        @step(name)
+        def _():
+            for chip_name in chips:
+                wait(*arrivals[chip_name])
+                if chip_name == (0, "y"):
+                    loads[1].wait()
+            acc[...] += mm(normed[k], wfull[k], ((1,), (0,)))
+
+    arrivals = {
+        (0, "y"): ("S0y",),
+        (0, "n"): ("SBy", "SAy"),
+        (2, "y"): ("SAq+", "SAq-", "SBq+", "SBq-"),
+        (2, "n"): ("SAyq+", "SAyq-", "SBoq+", "SBoq-"),
+    }
     for s, d in SIGN.items():
-        product(-d, "y", ("SA+" + s, "SA-" + s, "SB" + s))
-        product(-d, "n", ("SAy+" + s, "SAy-" + s, "SBo" + s))
-    product(2, "y", ("SAq+", "SAq-", "SBq+", "SBq-"))
-    product(2, "n", ("SAyq+", "SAyq-", "SBoq+", "SBoq-"))
+        arrivals[-d, "y"] = ("SA+" + s, "SA-" + s, "SB" + s)
+        arrivals[-d, "n"] = ("SAy+" + s, "SAy-" + s, "SBo" + s)
+    y0, y1, y9, y2 = (0, "y"), (1, "y"), (-1, "y"), (2, "y")
+    n0, n1, n9, n2 = (0, "n"), (1, "n"), (-1, "n"), (2, "n")
+    product("m0", pick(y1, y0, y0, y0), y0, y1)
+    product("m1", pick(y9, y2, y1, y1), y9, y2)
+    product("m2", pick(n0, n0, y9, y9), n0)
+    product("m3", pick(n1, n1, y2, y2), n1)
+    product("m4", pick(n9, n9, n1, n0), n9)
+    product("m5", pick(y0, y1, n0, n1))
+    product("m6", pick(y2, y9, n9, n9))
+    product("m7", pick(n2, n2, n2, n2), n2)
 
     def head(h):
         @step("att%d" % h)
@@ -651,8 +653,17 @@
 
 
 def hand_over(*refs):
-    for src, dst in zip(refs[:3], refs[3:]):
-        dst[...] = src[...]
+    src, dst, held, sem = refs[:3], refs[3:6], refs[6:9], refs[9]
+    order = (2, 1, 0)
+    loads = [pltpu.make_async_copy(src[i], held[i], sem.at[0, i]) for i in order]
+    stores = [pltpu.make_async_copy(held[i], dst[i], sem.at[1, i]) for i in order]
+    for cp in loads:
+        cp.start()
+    for load, cp in zip(loads, stores):
+        load.wait()
+        cp.start()
+    for cp in stores:
+        cp.wait()
 
 
 def per_device(tokens, w_qkv, out_grad):
@@ -710,12 +721,13 @@
             collective_id=0, has_side_effects=True, vmem_limit_bytes=62 * 1024 * 1024
         ),
     )(tokens, w_qkv, out_grad)
-    in_vmem = [pl.BlockSpec(memory_space=vmem)] * 3
     return pl.pallas_call(
         hand_over,
         out_shape=[jax.ShapeDtypeStruct(r.shape, r.dtype) for r in results],
-        in_specs=in_vmem,
-        out_specs=in_vmem,
+        in_specs=[pl.BlockSpec(memory_space=pltpu.HBM)] * 3,
+        out_specs=[pl.BlockSpec(memory_space=pltpu.HBM)] * 3,
+        scratch_shapes=[vmem(r.shape, r.dtype) for r in results]
+        + [pltpu.SemaphoreType.DMA((2, 3))],
     )(*results)
 
 

time: 90.7 us -> 90.5 us (level)
  no operation moved by 1% of the time
where the time goes in v4:
time: 90.5 us; the launch traced here: 90.4 us
  Pallas kernels  89.6 us (99%)
    pallas_call x1, Pallas kernels, per_device(): pl.pallas_call(kernel, out_shape=(jax.ShapeDtypeStruct(out_grad.shape, BF...  87.5 us
    pallas_call x1, Pallas kernels, per_device(): pl.pallas_call(hand_over, out_shape=[jax.ShapeDtypeStruct(r.shape, r.dtyp...  2.1 us

profile of v4, /device:TPU:1, one launch (start us, length us, event | category | flops | bytes accessed | tf_op | source)
XLA Modules:
  0.0 90.4 jit_solution(6011314979321302633)
XLA Ops:
  0.6 87.5 %shard_map.58 = (bf16[256,256]{1,0:T(8,128)(2,1)}, f32[256,384]{1,0:T(8,128)}, bf16[384,768]{1,0:T(8,128)(2,1)}) custom-call(bf16[256,384]{1,0:T(8,128)(2,1)} %tok_hbm.1, bf16[384,768]{1,0:T(8,128)(2,1)} %w_hbm.1, bf16[256,256]{1,0:T(8,128)(2,1)} %og_hbm.1), custom_call_target="tpu_custom_call" | custom-call | tf_op jit(solution)/shard_map/pallas_call | solution.py:710
  88.2 2.1 %shard_map.59 = (bf16[256,256]{1,0:T(8,128)(2,1)}, f32[256,384]{1,0:T(8,128)}, bf16[384,768]{1,0:T(8,128)(2,1)}) custom-call(bf16[256,256]{1,0:T(8,128)(2,1)} %get-tuple-element.6.refs_0_, f32[256,384]{1,0:T(8,128)} %get-tuple-element.7.refs_1_, bf16[384,768]{1,0:T(8,128)(2,1)} %get-tuple-element.8.refs_2_), custom_call_target="tpu_custom_call" | custom-call | tf_op jit(solution)/shard_map/pallas_call | solution.py:724

commit v5 on v4

--- a/solution.py
+++ b/solution.py
@@ -14,27 +14,27 @@
 OTHER = {"+": "-", "-": "+"}
 
 ORDER = (
-    87, 23, 7, 55, 37, 5, 1, 39, 56, 21,
-    24, 38, 57, 6, 8, 22, 0, 2, 88, 25,
-    11, 45, 59, 58, 62, 27, 75, 9, 73, 40,
-    41, 46, 60, 13, 29, 69, 66, 77, 63, 79,
-    48, 3, 30, 14, 52, 42, 35, 19, 47, 61,
-    4, 70, 67, 81, 31, 15, 26, 64, 83, 49,
-    12, 53, 43, 16, 32, 28, 71, 68, 85, 89,
-    143, 115, 141, 117, 105, 103, 133, 113, 135, 131,
-    33, 17, 50, 145, 10, 107, 65, 109, 36, 54,
-    137, 90, 91, 92, 93, 94, 18, 44, 111, 72,
-    34, 20, 51, 139, 96, 95, 97, 98, 187, 188,
-    99, 191, 178, 140, 189, 195, 194, 146, 148, 104,
-    170, 112, 171, 180, 100, 196, 164, 181, 134, 172,
-    138, 153, 142, 192, 182, 154, 147, 193, 174, 106,
-    167, 132, 173, 177, 116, 101, 184, 136, 166, 118,
-    120, 205, 114, 175, 199, 197, 185, 155, 126, 179,
-    163, 186, 190, 144, 150, 168, 108, 149, 156, 74,
-    76, 110, 119, 125, 165, 183, 122, 157, 128, 151,
-    78, 176, 207, 152, 121, 158, 80, 127, 201, 169,
-    124, 130, 198, 204, 82, 206, 200, 159, 123, 161,
-    84, 129, 86, 102, 203, 209, 160, 202, 208, 162,
+    39, 87, 24, 37, 56, 23, 8, 55, 38, 0,
+    21, 22, 57, 1, 2, 6, 5, 7, 88, 45,
+    59, 40, 62, 75, 29, 41, 73, 58, 46, 25,
+    60, 52, 27, 13, 48, 14, 63, 79, 9, 42,
+    77, 30, 69, 3, 11, 66, 47, 61, 31, 4,
+    53, 15, 49, 35, 26, 64, 19, 83, 43, 81,
+    28, 70, 67, 32, 10, 16, 54, 50, 12, 65,
+    44, 85, 89, 103, 135, 117, 107, 115, 36, 17,
+    71, 137, 33, 113, 105, 143, 68, 145, 131, 109,
+    111, 133, 141, 90, 91, 20, 92, 93, 94, 34,
+    51, 18, 72, 139, 95, 96, 97, 98, 187, 188,
+    99, 140, 192, 189, 194, 146, 112, 191, 173, 136,
+    163, 180, 195, 196, 104, 193, 118, 142, 148, 138,
+    153, 100, 114, 110, 154, 147, 125, 120, 174, 175,
+    171, 181, 182, 178, 134, 164, 165, 126, 184, 199,
+    197, 177, 108, 116, 101, 205, 119, 155, 166, 132,
+    106, 185, 186, 190, 179, 167, 170, 144, 168, 149,
+    156, 150, 172, 176, 122, 74, 127, 128, 121, 76,
+    183, 157, 158, 201, 207, 151, 152, 78, 169, 198,
+    204, 124, 129, 200, 206, 130, 123, 80, 161, 159,
+    82, 203, 209, 84, 86, 102, 162, 160, 202, 208,
 )
 
 

time: 90.5 us -> 92.8 us (1.025)
  Pallas kernels: 89.6 us -> 91.9 us
    pallas_call x1, Pallas kernels: 87.5 us -> 89.8 us  [per_device(): pl.pallas_call(kernel, out_shape=(jax.ShapeDtypeStruct(out_grad.shape, BF...]
where the time goes in v5:
time: 92.8 us; the launch traced here: 92.7 us
  Pallas kernels  91.9 us (99%)
    pallas_call x1, Pallas kernels, per_device(): pl.pallas_call(kernel, out_shape=(jax.ShapeDtypeStruct(out_grad.shape, BF...  89.8 us
    pallas_call x1, Pallas kernels, per_device(): pl.pallas_call(hand_over, out_shape=[jax.ShapeDtypeStruct(r.shape, r.dtyp...  2.1 us

profile of v5, /device:TPU:1, one launch (start us, length us, event | category | flops | bytes accessed | tf_op | source)
XLA Modules:
  0.0 92.7 jit_solution(2586893852017515296)
XLA Ops:
  0.6 89.8 %shard_map.58 = (bf16[256,256]{1,0:T(8,128)(2,1)}, f32[256,384]{1,0:T(8,128)}, bf16[384,768]{1,0:T(8,128)(2,1)}) custom-call(bf16[256,384]{1,0:T(8,128)(2,1)} %tok_hbm.1, bf16[384,768]{1,0:T(8,128)(2,1)} %w_hbm.1, bf16[256,256]{1,0:T(8,128)(2,1)} %og_hbm.1), custom_call_target="tpu_custom_call" | custom-call | tf_op jit(solution)/shard_map/pallas_call | solution.py:710
  90.4 2.1 %shard_map.59 = (bf16[256,256]{1,0:T(8,128)(2,1)}, f32[256,384]{1,0:T(8,128)}, bf16[384,768]{1,0:T(8,128)(2,1)}) custom-call(bf16[256,256]{1,0:T(8,128)(2,1)} %get-tuple-element.6.refs_0_, f32[256,384]{1,0:T(8,128)} %get-tuple-element.7.refs_1_, bf16[384,768]{1,0:T(8,128)(2,1)} %get-tuple-element.8.refs_2_), custom_call_target="tpu_custom_call" | custom-call | tf_op jit(solution)/shard_map/pallas_call | solution.py:724
